TPU v7x, 256 devices: a whole 4x4x8 slice. The times are simulated.
256 devices in a mesh: tenant: 8 (over z), replica: 4 (over x), row: 8 (over y, core).
Axes of the slice: x: 4, y: 4, z: 8, core: 2. Of those that a mesh axis runs over, the one named last changes fastest.
Arguments:
- acts: bfloat16 [8192, 8192], P('row', 'replica'), may hold values from -6 to 6
- base_weight: bfloat16 [8192, 8192], P('replica', 'tenant'), may hold values from -0.0625 to 0.0625
- delta_blocks: bfloat16 [16, 208, 128, 128], P('tenant', 'replica'), may hold values from -0.25 to 0.25
- block_index: int32 [16, 208], P('tenant', 'replica'), may hold values from 0 to 1023, as said below
- tenant_counts: int32 [8, 16], P('row'), may hold values from 1 to 256, as said below
Outputs:
- projected: bfloat16 [8192, 8192], P('row', ('tenant', 'replica'))
Inputs may be any that keep to these rules, and one draw needn't show every extreme that they name: Each row of tenant_counts sums to 1024; exactly one entry of each row equals 256, and at least one equals 1. `block_index`: the 52 entries of one tenant and one quarter (entries q * 52 to (q + 1) * 52 - 1) are distinct.
All inputs are finite; a program needn't handle non-finite values.
Results may differ from a plain program's by a relative error of at most 0.015.
Values may be sent and summed in bfloat16 or wider, within the bound.
A program may use at most 192 MiB of HBM per device.

v0:
```python
import jax
import jax.numpy as jnp
from jax import lax
from jax.sharding import PartitionSpec as P

CAP = 256


def body(acts, base_weight, delta_blocks, block_index, tenant_counts):
    rows, quarter = acts.shape
    tenants_dev, nbr = block_index.shape
    n_rep = lax.axis_size("replica")
    width = quarter * n_rep
    nbc = width // 128
    bq = quarter // 128
    capacity = CAP
    counts = tenant_counts[0]
    offsets = jnp.cumsum(counts) - counts
    tenant_here = lax.axis_index("tenant")
    slots = jnp.arange(capacity, dtype=jnp.int32)
    base_part = lax.psum_scatter(
        lax.dot_general(
            base_weight, acts, (((0,), (1,)), ((), ())), preferred_element_type=jnp.float32
        ).astype(jnp.bfloat16),
        "replica",
        scatter_dimension=0,
        tiled=True,
    ).astype(jnp.float32)
    shares = []
    targets = []
    for local_tenant in range(tenants_dev):
        tenant_id = tenant_here * tenants_dev + local_tenant
        start = offsets[tenant_id]
        count = counts[tenant_id]
        rowid = jnp.minimum(start + slots, rows - 1)
        picked = jnp.take(acts, rowid, axis=0)
        positions = block_index[local_tenant]
        brow = positions // nbc
        bcol = positions % nbc
        tiles = picked.reshape(capacity, bq, 128)
        chosen = jnp.take(tiles, brow, axis=1)
        contrib = jnp.einsum(
            "cnk,nkl->cnl", chosen, delta_blocks[local_tenant], preferred_element_type=jnp.float32
        )
        onehot = (bcol[:, None] == jnp.arange(nbc, dtype=jnp.int32)[None, :]).astype(jnp.float32)
        share = jnp.einsum("cnl,nb->cbl", contrib, onehot, precision=lax.Precision.HIGHEST).reshape(
            capacity, width
        )
        valid = slots < count
        share = jnp.where(valid[:, None], share, 0.0).astype(jnp.bfloat16)
        shares.append(lax.optimization_barrier(share))
        targets.append(jnp.where(valid, start + slots, rows))
    partial_value = jnp.zeros((rows, width), jnp.bfloat16)
    for share, target in zip(shares, targets):
        partial_value = partial_value.at[target].set(share, mode="drop")
    summed = lax.psum_scatter(
        partial_value, ("tenant", "replica"), scatter_dimension=1, tiled=True
    ).astype(jnp.float32)
    return (base_part.T + summed).astype(jnp.bfloat16)


def solution(mesh):
    placed = (
        P("row", "replica"),
        P("replica", "tenant"),
        P("tenant", "replica", None, None),
        P("tenant", "replica"),
        P("row", None),
    )
    return jax.shard_map(
        body, mesh=mesh, in_specs=placed, out_specs=P("row", ("tenant", "replica")), check_vma=False
    )
```

profile of v0, /device:TPU:1, one launch (start us, length us, event | category | flops | bytes accessed | tf_op | source)
XLA Modules:
  0.0 408.3 jit_solution(17728383317556881311)
XLA Ops:
  6.5 9.3 %convolution_convert_fusion = bf16[1024,1024]{1,0:T(8,128)(2,1)} fusion(bf16[2048,1024]{1,0:T(8,128)(2,1)} %param.10, bf16[1024,2048]{1,0:T(8,128)(2,1)} %param.9), kind=kOutput, calls=%fused_computation.26 | convolution fusion | flops 4296015872 | bytes 10485760 | tf_op jit(solution)/shard_map/dot_general | solution.py:22
  18.5 0.6 constant_dynamic-slice_fusion
  19.1 5.1 %gather_fusion = bf16[256,2048]{1,0:T(8,128)(2,1)S(1)} fusion(bf16[1024,2048]{1,0:T(8,128)(2,1)} %param.9, s32[1024]{0:T(1024)S(1)} %pad_clamp_fusion.3), kind=kCustom, calls=%fused_computation.clone | custom fusion | bytes 2098176 | tf_op jit(solution)/shard_map/jit(_take)/gather | solution.py:36
  24.2 0.6 iota_compare_fusion.3
  25.2 2.8 gather_fusion.1
  28.0 3.6 fusion.12
  31.6 11.3 %fusion.6 = bf16[64,256,128]{2,0,1:T(8,128)(2,1)S(1)} fusion(f32[52,256,128]{2,1,0:T(8,128)S(1)} %fusion.12, s32[52]{0:T(128)S(1)} %get-tuple-element.17), kind=kOutput, calls=%fused_computation.14 | convolution fusion | flops 1308626176 | bytes 11010256 | tf_op jit(solution)/shard_map/cnl,nb->cbl/dot_general | solution.py:46
  42.9 10.4 %fusion.1 = bf16[256,8192]{1,0:T(8,128)(2,1)} fusion(bf16[32,8,64,128]{3,2,1,0:T(8,128)(2,1)S(1)} %bitcast.91, pred[256]{0:T(512)(128)(4,1)S(1)} %iota_compare_fusion.3), kind=kLoop, calls=%fused_computation.9 | loop fusion | flops 2097152 | bytes 8388864 | tf_op jit(solution)/shard_map/convert_element_type | solution.py:50
  53.3 0.6 compare_select_fusion.2
  54.0 5.1 %gather_fusion.2 = bf16[256,2048]{1,0:T(8,128)(2,1)S(1)} fusion(bf16[1024,2048]{1,0:T(8,128)(2,1)} %param.9, s32[1024]{0:T(1024)S(1)} %pad_clamp_fusion.1), kind=kCustom, calls=%fused_computation.2.clone | custom fusion | bytes 2098176 | tf_op jit(solution)/shard_map/jit(_take)/gather | solution.py:36
  59.1 0.7 compare_and_fusion.1
  60.1 3.2 gather_fusion.3
  63.3 0.6 iota_compare_fusion.2
  63.9 3.6 fusion.10
  67.5 11.1 %fusion.4 = bf16[64,256,128]{2,0,1:T(8,128)(2,1)S(1)} fusion(f32[52,256,128]{2,1,0:T(8,128)S(1)} %fusion.10, s32[52]{0:T(128)S(1)} %get-tuple-element.6), kind=kOutput, calls=%fused_computation.12 | convolution fusion | flops 1308626176 | bytes 11010256 | tf_op jit(solution)/shard_map/cnl,nb->cbl/dot_general | solution.py:46
  78.6 10.5 %fusion = bf16[256,8192]{1,0:T(8,128)(2,1)} fusion(bf16[32,8,64,128]{3,2,1,0:T(8,128)(2,1)S(1)} %bitcast.92, pred[256]{0:T(512)(128)(4,1)S(1)} %iota_compare_fusion.2), kind=kLoop, calls=%fused_computation.7 | loop fusion | flops 2097152 | bytes 8388864 | tf_op jit(solution)/shard_map/convert_element_type | solution.py:50
  89.1 1.2 compare_select_fusion.1
  90.3 17.0 %scatter_custom_fusion = bf16[1024,8192]{1,0:T(8,128)(2,1)} fusion(s32[256]{0:T(256)S(1)} %bitcast.95, bf16[256,8192]{1,0:T(8,128)(2,1)} %fusion.1, bf16[]{:T(256)} %constant.74.clone.1), kind=kCustom, calls=%fused_computation.10 | custom fusion | bytes 16777728 | tf_op jit(solution)/shard_map/scatter | solution.py:55
  107.4 1.3 compare_select_fusion
  108.6 22.7 %scatter_fusion = bf16[1024,8192]{1,0:T(8,128)(2,1)} fusion(bf16[1024,8192]{1,0:T(8,128)(2,1)} %scatter_custom_fusion, s32[256]{0:T(256)S(1)} %bitcast.94, bf16[256,8192]{1,0:T(8,128)(2,1)} %fusion), kind=kCustom, calls=%fused_computation.5 | custom fusion | bytes 12583936 | tf_op jit(solution)/shard_map/scatter | solution.py:55
  131.3 22.4 %copy.13 = bf16[1024,8192]{0,1:T(8,128)(2,1)} copy(bf16[1024,8192]{1,0:T(8,128)(2,1)} %scatter_fusion) | data formatting | bytes 33554432 | tf_op jit(solution)/shard_map/scatter | solution.py:55
  153.8 245.0 %reduce-scatter.5.cloned.1.call-done = bf16[1024,256]{0,1:T(8,128)(2,1)} async-done(((bf16[1024,8192]{0,1:T(8,128)(2,1)}), bf16[1024,256]{0,1:T(8,128)(2,1)}) %reduce-scatter.5.cloned.1.call-update) | async-done | bytes 524304 | tf_op jit(solution)/shard_map/reduce_scatter | solution.py:56
  398.8 1.4 fusion.24
  400.2 1.0 copy.14
  (23 shorter events, 3.3 us)
Async XLA Ops:
  6.5 9.9 %copy-start = (s32[1,16]{1,0:T(1,128)S(1)}, s32[1,16]{1,0:T(1,128)}, u32[]{:S(2)}) copy-start(s32[1,16]{1,0:T(1,128)} %param.13) | copy-start | bytes 196
  6.5 147.3 %reduce-scatter.3.cloned.1.call-start = ((), (), s32[]{:S(2)}) async-start(), calls=%async_computation.2 | async-start | bytes 2621440 | tf_op jit(solution)/shard_map/reduce_scatter | solution.py:21
  15.9 382.9 %reduce-scatter.5.cloned.1.call-start = ((), (), s32[]{:S(2)}) async-start(), calls=%async_computation.3 | async-start | bytes 17301504 | tf_op jit(solution)/shard_map/reduce_scatter | solution.py:56
  19.1 5.1 %copy-start.1 = (s32[2,52]{1,0:T(2,128)S(1)}, s32[2,52]{1,0:T(2,128)}, u32[]{:S(2)}) copy-start(s32[2,52]{1,0:T(2,128)} %param.12) | copy-start | bytes 1252
Sparse Core Ops, SparseCore 0:
  16.0 36.1 reduce-scatter.2
  153.9 244.8 reduce-scatter.4
where the time goes:
time: 416 us; the launch traced here: 408 us
  waiting for transfers between devices  245 us (59%)
  local copies, waits for them, and re-layouts  80.6 us (19%)
  matrix products  38.8 us (9%)
  other arithmetic  29.4 us (7%)
  between operations  13.9 us (3%)
    reduce_scatter x1, waiting for transfers between devices, body(): lax.psum_scatter(partial_value, ('tenant', 'replica'), scatter_dimension=...  245 us
    scatter x3, local copies, waits for them, and re-layouts, body(): partial_value = partial_value.at[target].set(share, mode='drop')  62.2 us
    dot_general x2, matrix products, body(): jnp.einsum('cnl,nb->cbl', contrib, onehot, precision=lax.Precision.HIGHEST)  22.4 us
    convert_element_type x2, other arithmetic, body(): share = jnp.where(valid[:, None], share, 0.0).astype(jnp.bfloat16)  20.9 us
    gather x2, local copies, waits for them, and re-layouts, body(): picked = jnp.take(acts, rowid, axis=0)  10.2 us
    dot_general x1, matrix products, body(): lax.dot_general(base_weight, acts, (((0,), (1,)), ((), ())), preferred_el...  9.33 us
  transfers between devices with their start and end apart: 2, of which 1 were waited for; matrix products, arithmetic and copies ran while one was open for 34% of the time, Pallas kernels for 0%

commit v1 on v0

v1 whole, which is shorter than its diff:
```python
import functools

import jax
import jax.numpy as jnp
from jax import lax
from jax.experimental import pallas as pl
from jax.experimental.pallas import tpu as pltpu
from jax.sharding import PartitionSpec as P

SLOTS = 28
COUNT = 127
OFFSETS = (1, 7, 2, 6, 3, 5, 4)
MESH = pl.DeviceIdType.MESH
MIB = 1 << 20


def pack_kernel(round_ref, index_ref, delta_ref, send_ref, lists_ref, slab, sem):
    part = lax.axis_index("row")
    load = pltpu.make_async_copy(
        delta_ref.at[:, pl.ds(pl.multiple_of(part * 16, 16), 16), :], slab, sem
    )
    load.start()
    first = round_ref[0] * SLOTS
    for dest in range(8):
        lists_ref[dest, COUNT] = 0
    load.wait()
    tenants, tiles = index_ref.shape
    for tenant in range(tenants):

        def place(n, carry):
            where = index_ref[tenant, n]
            dest = lax.shift_right_logical(where & 63, 3)
            count = lists_ref[dest, COUNT]
            tile = tenant * tiles + n
            lists_ref[dest, count] = where + tenant * 1024 + tile * 2048
            lists_ref[dest, COUNT] = count + 1
            slot = count - first
            slot = jnp.where((slot >= 0) & (slot < SLOTS), slot, SLOTS)
            send_ref[dest, slot] = slab[tile]
            return carry

        lax.fori_loop(0, tiles, place, 0)


def pack(step, block_index, delta):
    return pl.pallas_call(
        pack_kernel,
        out_shape=(
            jax.ShapeDtypeStruct((8, SLOTS + 1, 16, 128), jnp.bfloat16),
            jax.ShapeDtypeStruct((8, 128), jnp.int32),
        ),
        in_specs=[
            pl.BlockSpec(memory_space=pltpu.SMEM),
            pl.BlockSpec(memory_space=pltpu.SMEM),
            pl.BlockSpec(memory_space=pl.ANY),
        ],
        out_specs=(
            pl.BlockSpec(memory_space=pltpu.VMEM),
            pl.BlockSpec(memory_space=pltpu.SMEM),
        ),
        scratch_shapes=[
            pltpu.VMEM((delta.shape[0], 16, 128), jnp.bfloat16),
            pltpu.SemaphoreType.DMA,
        ],
        name="pack_tiles",
    )(step, block_index, delta)


def exchange_kernel(with_base, *refs):
    if with_base:
        send, lists, acts, weight, recv, all_lists, base = refs[:7]
        rest = refs[7:]
        acts_v, weight_v, base_v, load_sem, store_sem = rest[-5:]
    else:
        send, lists, recv, all_lists = refs[:4]
        rest = refs[4:]
    (z_s, z_r, l_s, l_r, own_sem, up_s, up_r, dn_s, dn_r, fu_s, fu_r, fd_s, fd_r, co_s, co_r) = rest[:15]
    t = lax.axis_index("tenant")
    part = lax.axis_index("row")
    core = part % 2
    y = part // 2
    up = ((y + 1) % 4) * 2 + core
    down = ((y + 3) % 4) * 2 + core
    far = ((y + 2) % 4) * 2 + core
    twin = y * 2 + (1 - core)
    half = SLOTS // 2

    if with_base:
        loads = [
            pltpu.make_async_copy(weight, weight_v, load_sem.at[0]),
            pltpu.make_async_copy(acts, acts_v, load_sem.at[1]),
        ]
        for load in loads:
            load.start()
    own = pltpu.make_async_copy(lists, all_lists.at[t], own_sem)
    own.start()

    barrier = pltpu.get_barrier_semaphore()
    for k in OFFSETS:
        pl.semaphore_signal(barrier, inc=1, device_id={"tenant": (t + k) % 8}, device_id_type=MESH)
    for other in (up, down, twin):
        pl.semaphore_signal(barrier, inc=1, device_id={"row": other}, device_id_type=MESH)
    pl.semaphore_wait(barrier, 10)

    def remote(src, dst, s, r, who):
        return pltpu.make_async_remote_copy(
            src_ref=src, dst_ref=dst, send_sem=s, recv_sem=r, device_id=who, device_id_type=MESH
        )

    z_copies = []
    for i, k in enumerate(OFFSETS):
        dest = (t + k) % 8
        copy = remote(
            send.at[dest, pl.ds(0, SLOTS)], recv.at[t, part], z_s.at[i], z_r.at[i], {"tenant": dest}
        )
        copy.start()
        z_copies.append(copy)
    for i, k in enumerate(OFFSETS):
        copy = remote(lists, all_lists.at[t], l_s.at[i], l_r.at[i], {"tenant": (t + k) % 8})
        copy.start()
        z_copies.append(copy)

    sent = []
    up_c, dn_c, fu_c, fd_c, co_c = {}, {}, {}, {}, {}

    def go(copy):
        copy.start()
        sent.append(copy)
        return copy

    for i in range(9):
        if i < 7:
            src = (t - OFFSETS[i] + 8) % 8
            z_copies[i].wait_recv()
            block = recv.at[src, part]
            up_c[i] = go(remote(block, block, up_s.at[i], up_r.at[i], {"row": up}))
            dn_c[i] = go(remote(block, block, dn_s.at[i], dn_r.at[i], {"row": down}))
            co_c[i, 0] = go(remote(block, block, co_s.at[i, 0], co_r.at[i, 0], {"row": twin}))
        j = i - 1
        if 0 <= j < 7:
            src = (t - OFFSETS[j] + 8) % 8
            up_c[j].wait_recv()
            block = recv.at[src, down]
            piece = recv.at[src, down, pl.ds(0, half)]
            fu_c[j] = go(remote(piece, piece, fu_s.at[j], fu_r.at[j], {"row": up}))
            co_c[j, 1] = go(remote(block, block, co_s.at[j, 1], co_r.at[j, 1], {"row": twin}))
            dn_c[j].wait_recv()
            block = recv.at[src, up]
            piece = recv.at[src, up, pl.ds(half, SLOTS - half)]
            fd_c[j] = go(remote(piece, piece, fd_s.at[j], fd_r.at[j], {"row": down}))
            co_c[j, 2] = go(remote(block, block, co_s.at[j, 2], co_r.at[j, 2], {"row": twin}))
        j = i - 2
        if 0 <= j < 7:
            src = (t - OFFSETS[j] + 8) % 8
            fu_c[j].wait_recv()
            fd_c[j].wait_recv()
            block = recv.at[src, far]
            co_c[j, 3] = go(remote(block, block, co_s.at[j, 3], co_r.at[j, 3], {"row": twin}))
        if with_base and i < 4:
            if i == 0:
                for load in loads:
                    load.wait()
            rows = pl.ds(i * 256, 256)

            @pl.loop(0, 4)
            def _(c):
                out = jnp.dot(
                    acts_v[rows, :],
                    weight_v[:, pl.ds(pl.multiple_of(c * 256, 256), 256)],
                    preferred_element_type=jnp.float32,
                )
                base_v[2 * c, rows, :] = out[:, :128]
                base_v[2 * c + 1, rows, :] = out[:, 128:]

            if i == 3:
                store = pltpu.make_async_copy(base_v, base, store_sem)
                store.start()
    for i in range(7):
        for n in range(4):
            co_c[i, n].wait_recv()
    for i in range(7, 14):
        z_copies[i].wait_recv()
    for copy in z_copies + sent:
        copy.wait_send()
    own.wait()
    if with_base:
        store.wait()


def exchange(send, lists, acts=None, weight=None):
    with_base = acts is not None
    sems = [pltpu.SemaphoreType.DMA((7,))] * 4 + [pltpu.SemaphoreType.DMA]
    sems += [pltpu.SemaphoreType.DMA((7,))] * 8 + [pltpu.SemaphoreType.DMA((7, 4))] * 2
    out_shape = [
        jax.ShapeDtypeStruct((8, 8, SLOTS, 16, 128), jnp.bfloat16),
        jax.ShapeDtypeStruct((8, 8, 128), jnp.int32),
    ]
    operands = [send, lists]
    if with_base:
        rows, depth = acts.shape
        columns = weight.shape[1]
        operands += [acts, weight]
        out_shape.append(jax.ShapeDtypeStruct((columns // 128, rows, 128), jnp.float32))
        sems += [
            pltpu.VMEM((rows, depth), jnp.bfloat16),
            pltpu.VMEM((depth, columns), jnp.bfloat16),
            pltpu.VMEM((columns // 128, rows, 128), jnp.float32),
            pltpu.SemaphoreType.DMA((2,)),
            pltpu.SemaphoreType.DMA,
        ]
    return pl.pallas_call(
        functools.partial(exchange_kernel, with_base),
        out_shape=tuple(out_shape),
        in_specs=[pl.BlockSpec(memory_space=pl.ANY)] * len(operands),
        out_specs=tuple([pl.BlockSpec(memory_space=pl.ANY)] * len(out_shape)),
        scratch_shapes=sems,
        compiler_params=pltpu.CompilerParams(
            collective_id=0 if with_base else 1,
            has_side_effects=True,
            vmem_limit_bytes=(24 if with_base else 4) * MIB,
        ),
        name="exchange_tiles_base" if with_base else "exchange_tiles",
    )(*operands)


GROUP = 4
CHUNK = 128


def delta_kernel(
    first_round, round_ref, lists_ref, counts_ref, acts, delta, recv, start_ref, out_ref,
    offsets, acts_v, own_v, recv_v, acc, sems,
):
    t = lax.axis_index("tenant")
    low = round_ref[0] * SLOTS
    loads = [pltpu.make_async_copy(acts, acts_v, sems.at[0])]
    if first_round:
        loads.append(pltpu.make_async_copy(start_ref, acc, sems.at[9]))
        loads.append(pltpu.make_async_copy(delta, own_v, sems.at[8]))
    for k in range(1, 8):
        loads.append(pltpu.make_async_copy(recv.at[(t + k) % 8], recv_v.at[k], sems.at[k]))
    for load in loads:
        load.start()
    total = jnp.int32(0)
    for tenant in range(16):
        offsets[tenant] = total
        total = total + counts_ref[0, tenant]
    rows = acts_v.shape[0]
    if not first_round:
        for d in range(4):
            acc[2 * d] = start_ref[d, :, :128].astype(jnp.float32)
            acc[2 * d + 1] = start_ref[d, :, 128:].astype(jnp.float32)

    line = lax.broadcasted_iota(jnp.int32, (CHUNK, 128), 0)

    def apply(src, count, begin, tile_of):
        def group(g, carry):
            work = []
            chunks = jnp.int32(0)
            for u in range(GROUP):
                j = g * GROUP + u
                valid = j < count
                j = jnp.minimum(j, count - 1)
                entry = lists_ref[src, t, begin + j]
                tenant = 2 * src + (lax.shift_right_logical(entry, 10) & 1)
                brow = lax.shift_right_logical(entry, 6) & 15
                bcol = entry & 7
                lo = offsets[tenant]
                hi = jnp.where(valid, lo + counts_ref[0, tenant], 0)
                base = lax.shift_right_logical(lo, 4) * 16
                chunks = jnp.maximum(chunks, lax.shift_right_arithmetic(hi - base + CHUNK - 1, 7))
                work.append((j, entry, brow, bcol, lo, hi, base))

            def chunk(i, carry):
                products = []
                for j, entry, brow, bcol, lo, hi, base in work:
                    at = pl.multiple_of(jnp.minimum(base + i * CHUNK, rows - CHUNK), 16)
                    x = acts_v[pl.ds(at, CHUNK), pl.ds(pl.multiple_of(brow * 128, 128), 128)]
                    out = jnp.dot(x, tile_of(j, entry), preferred_element_type=jnp.float32)
                    products.append((at, jnp.maximum(lo, base + i * CHUNK), hi, bcol, out))
                for at, lo, hi, bcol, out in products:
                    keep = (line >= lo - at) & (line < hi - at)
                    acc[bcol, pl.ds(at, CHUNK), :] += jnp.where(keep, out, 0.0)
                return carry

            lax.fori_loop(0, chunks, chunk, 0)
            return carry

        lax.fori_loop(0, lax.shift_right_logical(count + GROUP - 1, 2), group, 0)

    for load in loads[: 3 if first_round else 1]:
        load.wait()
    if first_round:
        apply(t, lists_ref[t, t, COUNT], 0, lambda j, entry: own_v[lax.shift_right_logical(entry, 11)])
    for k in range(1, 8):
        src = (t + k) % 8
        loads[(2 if first_round else 0) + k].wait()
        count = jnp.clip(lists_ref[src, t, COUNT] - low, 0, SLOTS)
        apply(src, count, low, lambda j, entry, k=k: recv_v[k, :, j].reshape(128, 128))

    @pl.loop(0, 8)
    def _(i):
        span = pl.ds(pl.multiple_of(i * 128, 128), 128)
        for d in range(4):
            out_ref[d, span, :128] = acc[2 * d, span, :].astype(jnp.bfloat16)
            out_ref[d, span, 128:] = acc[2 * d + 1, span, :].astype(jnp.bfloat16)


def add_delta(step, all_lists, counts, acts, delta, recv, start, first_round):
    rows, depth = acts.shape
    any_spec = pl.BlockSpec(memory_space=pl.ANY)
    smem = pl.BlockSpec(memory_space=pltpu.SMEM)
    vmem = pl.BlockSpec(memory_space=pltpu.VMEM)
    return pl.pallas_call(
        functools.partial(delta_kernel, first_round),
        out_shape=jax.ShapeDtypeStruct((4, rows, 256), jnp.bfloat16),
        in_specs=[smem, smem, smem, any_spec, any_spec, any_spec, any_spec if first_round else vmem],
        out_specs=vmem,
        scratch_shapes=[
            pltpu.SMEM((16,), jnp.int32),
            pltpu.VMEM((rows, depth), jnp.bfloat16),
            pltpu.VMEM(delta.shape, jnp.bfloat16),
            pltpu.VMEM(recv.shape, jnp.bfloat16),
            pltpu.VMEM((8, rows, 128), jnp.float32),
            pltpu.SemaphoreType.DMA((10,)),
        ],
        compiler_params=pltpu.CompilerParams(vmem_limit_bytes=40 * MIB),
        name="add_delta",
    )(step, all_lists, counts, acts, delta, recv, start)


PIECES = 4


def reduce_kernel(
    part, out_ref, mine, in_a, in_b, f_a, f_b, g_a, g_b, s_a, s_b, load_sem, send_sem, recv_sem
):
    me = lax.axis_index("replica")
    right, left, far = (me + 1) % 4, (me + 3) % 4, (me + 2) % 4
    half = part.shape[1] // 2
    size = half // PIECES

    loads = [
        pltpu.make_async_copy(part.at[right, pl.ds(0, half)], mine.at[0], load_sem.at[0]),
        pltpu.make_async_copy(part.at[left, pl.ds(half, half)], mine.at[1], load_sem.at[1]),
        pltpu.make_async_copy(part.at[me, pl.ds(0, half)], mine.at[2], load_sem.at[2]),
        pltpu.make_async_copy(part.at[me, pl.ds(half, half)], mine.at[3], load_sem.at[3]),
    ]
    for load in loads:
        load.start()
    barrier = pltpu.get_barrier_semaphore()
    for who in (right, left):
        pl.semaphore_signal(barrier, inc=1, device_id={"replica": who}, device_id_type=MESH)
    pl.semaphore_wait(barrier, 2)

    started = []

    def send(kind, piece, src, dst, who):
        copy = pltpu.make_async_remote_copy(
            src_ref=src,
            dst_ref=dst,
            send_sem=send_sem.at[kind, piece],
            recv_sem=recv_sem.at[kind, piece],
            device_id={"replica": who},
            device_id_type=MESH,
        )
        copy.start()
        started.append(copy)
        return copy

    ins_a, ins_b, fs_a, fs_b, gs_a, gs_b = [], [], [], [], [], []
    for p in range(PIECES):
        span = pl.ds(p * size, size)
        low, high = pl.ds(p * size, size), pl.ds(half + p * size, size)
        ins_a.append(send(0, p, part.at[far, low], in_a.at[span], right))
        ins_b.append(send(1, p, part.at[far, high], in_b.at[span], left))
    for p in range(PIECES):
        span = pl.ds(p * size, size)
        low, high = pl.ds(p * size, size), pl.ds(half + p * size, size)
        fs_b.append(send(2, p, part.at[right, high], f_b.at[span], right))
        fs_a.append(send(3, p, part.at[left, low], f_a.at[span], left))
    loads[0].wait()
    loads[1].wait()
    for p in range(PIECES):
        span = pl.ds(p * size, size)
        ins_a[p].wait_recv()
        s_a[span, :] = (mine[0, span, :].astype(jnp.float32) + in_a[span, :].astype(jnp.float32)).astype(jnp.bfloat16)
        gs_a.append(send(4, p, s_a.at[span], g_a.at[span], right))
        ins_b[p].wait_recv()
        s_b[span, :] = (mine[1, span, :].astype(jnp.float32) + in_b[span, :].astype(jnp.float32)).astype(jnp.bfloat16)
        gs_b.append(send(5, p, s_b.at[span], g_b.at[span], left))
    loads[2].wait()
    loads[3].wait()
    for p in range(PIECES):
        span = pl.ds(p * size, size)
        fs_a[p].wait_recv()
        gs_a[p].wait_recv()
        out_ref[pl.ds(p * size, size), :] = (
            mine[2, span, :].astype(jnp.float32) + f_a[span, :].astype(jnp.float32) + g_a[span, :].astype(jnp.float32)
        ).astype(jnp.bfloat16)
        fs_b[p].wait_recv()
        gs_b[p].wait_recv()
        out_ref[pl.ds(half + p * size, size), :] = (
            mine[3, span, :].astype(jnp.float32) + f_b[span, :].astype(jnp.float32) + g_b[span, :].astype(jnp.float32)
        ).astype(jnp.bfloat16)
    for copy in started:
        copy.wait_send()


def reduce_blocks(part):
    _, rows, columns = part.shape
    half = rows // 2
    return pl.pallas_call(
        reduce_kernel,
        out_shape=jax.ShapeDtypeStruct((rows, columns), jnp.bfloat16),
        in_specs=[pl.BlockSpec(memory_space=pl.ANY)],
        out_specs=pl.BlockSpec(memory_space=pltpu.VMEM),
        scratch_shapes=[pltpu.VMEM((4, half, columns), jnp.bfloat16)]
        + [pltpu.VMEM((half, columns), jnp.bfloat16)] * 8
        + [
            pltpu.SemaphoreType.DMA((4,)),
            pltpu.SemaphoreType.DMA((6, PIECES)),
            pltpu.SemaphoreType.DMA((6, PIECES)),
        ],
        compiler_params=pltpu.CompilerParams(
            collective_id=2, has_side_effects=True, vmem_limit_bytes=16 * MIB
        ),
        name="reduce_blocks",
    )(part)


def body(acts, base_weight, delta_blocks, block_index, tenant_counts):
    delta = delta_blocks.reshape(-1, 128, 128)
    here = lax.axis_index("tenant")
    step = jnp.zeros((1,), jnp.int32)
    send, lists = pack(step, block_index, delta)
    lengths = jnp.where(jnp.arange(8) == here, 0, lists[:, COUNT])
    longest = lax.pmax(jnp.max(lengths), ("tenant", "replica"))
    recv, all_lists, base = exchange(send, lists, acts, base_weight)
    part = add_delta(step, all_lists, tenant_counts, acts, delta, recv, base, True)

    def another(n, part):
        step = jnp.full((1,), n, jnp.int32)
        send, lists = pack(step, block_index, delta)
        recv, all_lists = exchange(send, lists)
        return add_delta(step, all_lists, tenant_counts, acts, delta, recv, part, False)

    part = lax.fori_loop(1, (longest + SLOTS - 1) // SLOTS, another, part)
    return reduce_blocks(part)


def solution(mesh):
    placed = (
        P("row", "replica"),
        P("replica", "tenant"),
        P("tenant", "replica", None, None),
        P("tenant", "replica"),
        P("row", None),
    )
    return jax.shard_map(
        body, mesh=mesh, in_specs=placed, out_specs=P("row", ("tenant", "replica")), check_vma=False
    )
```

time: 416 us -> 116 us (0.28); the launches traced: 408 us -> 116 us
  waiting for transfers between devices: 245 us -> 0 us
  Pallas kernels: 0 us -> 87.9 us
  local copies, waits for them, and re-layouts: 80.6 us -> 5.74 us
  matrix products: 38.8 us -> 0 us
  other arithmetic: 29.4 us -> 0.71 us
  blocking collectives: 0 us -> 20.4 us
  between operations: 13.9 us -> 0.82 us
    reduce_scatter x2 -> x0, waiting for transfers between devices: 245 us -> none  [the longest x1 245 us: body(): lax.psum_scatter(partial_value, ('tenant', 'replica'), scatter_dimension=...]
    pallas_call x0 -> x4, Pallas kernels: none -> 87.9 us  [the longest x1 47.7 us: exchange(): pl.pallas_call(functools.partial(exchange_kernel, with_base), out_shape=t...]
    scatter x3 -> x0, local copies, waits for them, and re-layouts: 62.2 us -> none  [body(): partial_value = partial_value.at[target].set(share, mode='drop')]
    dot_general x5 -> x0, matrix products: 38.8 us -> none  [the longest x2 22.4 us: body(): jnp.einsum('cnl,nb->cbl', contrib, onehot, precision=lax.Precision.HIGHEST)]
    convert_element_type x3 -> x0, other arithmetic: 22.3 us -> none  [the longest x2 20.9 us: body(): share = jnp.where(valid[:, None], share, 0.0).astype(jnp.bfloat16)]
    pmax x0 -> x1, blocking collectives: none -> 20.4 us  [body(): longest = lax.pmax(jnp.max(lengths), ('tenant', 'replica'))]
    gather x4 -> x0, local copies, waits for them, and re-layouts: 16.2 us -> none  [the longest x2 10.2 us: body(): picked = jnp.take(acts, rowid, axis=0)]
    unnamed x4 -> x15, local copies, waits for them, and re-layouts: 0.01 us -> 4.87 us
  transfers between devices with their start and end apart: 2 -> 0, of which waited for: 1 -> 0; matrix products, arithmetic and copies ran while one was open for 34% -> 0% of each run, Pallas kernels for 0% -> 0%
where the time goes in v1:
time: 116 us
  Pallas kernels  87.9 us (76%)
  blocking collectives  20.4 us (18%)
  local copies, waits for them, and re-layouts  5.74 us (5%)
    pallas_call x1, Pallas kernels, exchange(): pl.pallas_call(functools.partial(exchange_kernel, with_base), out_shape=t...  47.7 us
    pallas_call x1, Pallas kernels, reduce_blocks(): pl.pallas_call(reduce_kernel, out_shape=jax.ShapeDtypeStruct((rows, colum...  21.3 us
    pmax x1, blocking collectives, body(): longest = lax.pmax(jnp.max(lengths), ('tenant', 'replica'))  20.4 us
    pallas_call x1, Pallas kernels, add_delta(): pl.pallas_call(functools.partial(delta_kernel, first_round), out_shape=ja...  14.6 us
    unnamed x15, local copies, waits for them, and re-layouts  4.87 us
    pallas_call x1, Pallas kernels, pack(): pl.pallas_call(pack_kernel, out_shape=(jax.ShapeDtypeStruct((8, SLOTS + 1...  4.29 us

profile of v1, /device:TPU:1, one launch (start us, length us, event | category | flops | bytes accessed | tf_op | source)
XLA Modules:
  0.0 115.6 jit_solution(5735909166045007317)
XLA Ops:
  0.0 4.3 %pack_tiles.2 = (bf16[8,29,16,128]{3,2,1,0:T(8,128)(2,1)}, s32[8,128]{1,0:T(8,128)}) custom-call(s32[1]{0:T(128)} %constant.20.clone.1.round_ref, s32[2,52]{1,0:T(2,128)} %index_ref.1, bf16[104,128,128]{2,1,0:T(8,128)(2,1)} %bitcast.4), custom_call_target="tpu_custom_call" | custom-call | tf_op jit(solution)/shard_map/pack_tiles/pallas_call | solution.py:46
  4.3 0.9 slice_reduce_fusion
  5.2 0.7 fusion
  5.9 20.4 %pmax.7 = s32[]{:T(128)} all-reduce(s32[]{:T(128)} %fusion), channel_id=1, replica_groups=mesh['tenant'=8,'replica'=4,'row'=8] {'tenant','replica'}, use_global_device_ids=true, to_apply=%region_1.2 | all-reduce | flops 1 | bytes 8 | tf_op jit(solution)/shard_map/pmax | solution.py:438
  27.1 0.0 copy-start.1
  27.1 2.2 %copy-done.1 = bf16[2048,1024]{1,0:T(8,128)(2,1)S(1)} copy-done((bf16[2048,1024]{1,0:T(8,128)(2,1)S(1)}, bf16[2048,1024]{1,0:T(8,128)(2,1)}, u32[]{:S(2)}) %copy-start.1) | copy-done | bytes 4194328
  29.2 0.0 copy-start.2
  29.2 1.2 %copy-done.2 = bf16[8,29,16,128]{3,2,1,0:T(8,128)(2,1)S(1)} copy-done((bf16[8,29,16,128]{3,2,1,0:T(8,128)(2,1)S(1)}, bf16[8,29,16,128]{3,2,1,0:T(8,128)(2,1)}, u32[]{:S(2)}) %copy-start.2) | copy-done | bytes 950296
  30.4 0.0 copy-start.4
  30.4 0.7 copy-done.4
  31.1 0.0 copy-start.5
  31.1 0.0 copy-start.6
  31.1 0.0 copy-start.8
  31.1 47.7 %exchange_tiles_base.1 = (bf16[8,8,28,16,128]{4,3,2,1,0:T(8,128)(2,1)S(1)}, s32[8,8,128]{2,1,0:T(8,128)S(1)}, f32[8,1024,128]{2,1,0:T(8,128)S(1)}) custom-call(bf16[8,29,16,128]{3,2,1,0:T(8,128)(2,1)S(1)} %copy-done.2, s32[8,128]{1,0:T(8,128)S(1)} %copy-done.4, bf16[1024,2048]{1,0:T(8,128)(2,1)} %acts.1, bf16[2048,1024]{1,0:T(8,128)(2,1)S(1)} %copy-done.1), custom_call_target="tpu_custom_call" | custom-call | tf_op jit(solution)/shard_map/exchange_tiles_base/pallas_call | solution.py:211
  78.9 0.0 copy-done.5
  78.9 0.0 copy-done.6
  78.9 0.0 copy-done.8
  78.9 0.0 copy-start.7
  78.9 14.6 %add_delta.2 = bf16[4,1024,256]{2,1,0:T(8,128)(2,1)} custom-call(s32[1]{0:T(128)} %constant.20.clone.1.round_ref, s32[8,8,128]{2,1,0:T(8,128)S(1)} %get-tuple-element.54.lists_ref, s32[1,16]{1,0:T(1,128)S(1)} %copy-done.8, bf16[1024,2048]{1,0:T(8,128)(2,1)S(1)} %copy-done.6, bf16[104,128,128]{2,1,0:T(8,128)(2,1)S(1)} %bitcast.6, ...), custom_call_target="tpu_custom_call" | custom-call | tf_op jit(solution)/shard_map/add_delta/pallas_call | solution.py:314
  93.5 0.0 copy-done.7
  93.5 21.3 %reduce_blocks.1 = bf16[1024,256]{1,0:T(8,128)(2,1)S(1)} custom-call(bf16[4,1024,256]{2,1,0:T(8,128)(2,1)} %get-tuple-element.57.part), custom_call_target="tpu_custom_call" | custom-call | tf_op jit(solution)/shard_map/reduce_blocks/pallas_call | solution.py:413
  114.8 0.8 copy.15
  (1 shorter events, 0.0 us)
Async XLA Ops:
  27.1 2.2 %copy-start.1 = (bf16[2048,1024]{1,0:T(8,128)(2,1)S(1)}, bf16[2048,1024]{1,0:T(8,128)(2,1)}, u32[]{:S(2)}) copy-start(bf16[2048,1024]{1,0:T(8,128)(2,1)} %refs_3_.1) | copy-start | bytes 12582916
  29.2 1.2 %copy-start.2 = (bf16[8,29,16,128]{3,2,1,0:T(8,128)(2,1)S(1)}, bf16[8,29,16,128]{3,2,1,0:T(8,128)(2,1)}, u32[]{:S(2)}) copy-start(bf16[8,29,16,128]{3,2,1,0:T(8,128)(2,1)} %get-tuple-element.52.refs_0_) | copy-start | bytes 2850820
  30.4 0.7 copy-start.4
  31.1 47.7 %copy-start.5 = (bf16[2,52,128,128]{3,2,1,0:T(8,128)(2,1)S(1)}, bf16[2,52,128,128]{3,2,1,0:T(8,128)(2,1)}, u32[]{:S(2)}) copy-start(bf16[2,52,128,128]{3,2,1,0:T(8,128)(2,1)} %param.9) | copy-start | bytes 10223620
  31.1 47.8 %copy-start.6 = (bf16[1024,2048]{1,0:T(8,128)(2,1)S(1)}, bf16[1024,2048]{1,0:T(8,128)(2,1)}, u32[]{:S(2)}) copy-start(bf16[1024,2048]{1,0:T(8,128)(2,1)} %acts.1) | copy-start | bytes 12582916
  31.1 47.8 %copy-start.8 = (s32[1,16]{1,0:T(1,128)S(1)}, s32[1,16]{1,0:T(1,128)}, u32[]{:S(2)}) copy-start(s32[1,16]{1,0:T(1,128)} %counts_ref.1) | copy-start | bytes 196
  78.9 14.6 %copy-start.7 = (s32[2,52]{1,0:T(2,128)S(1)}, s32[2,52]{1,0:T(2,128)}, u32[]{:S(2)}) copy-start(s32[2,52]{1,0:T(2,128)} %index_ref.1) | copy-start | bytes 1252

commit v2 on v0

v2 whole, which is shorter than its diff:
```python
import functools

import jax
import jax.numpy as jnp
from jax import lax
from jax.experimental import pallas as pl
from jax.experimental.pallas import tpu as pltpu
from jax.sharding import PartitionSpec as P

SLOTS = 28
HALF = SLOTS // 2
SPARE = 28
GATHERED = 7 * HALF + SPARE
STARTS = (0, 2 * HALF, 4 * HALF, 6 * HALF, 7 * HALF)
SIZES = (2 * HALF, 2 * HALF, 2 * HALF, HALF, SPARE)
COUNT = 127
AHEAD = 8
OFFSETS = (1, 7, 2, 6, 3, 5, 4)
MESH = pl.DeviceIdType.MESH
MIB = 1 << 20


def list_kernel(index_ref, lists_ref):
    tenants, tiles = index_ref.shape
    counts = (jnp.int32(0), jnp.int32(0))
    for tenant in range(tenants):

        def place(n, counts):
            where = index_ref[tenant, n]
            dest = lax.shift_right_logical(where & 63, 3)
            byte = (dest & 3) * 8
            first = dest < 4
            word = jnp.where(first, counts[0], counts[1])
            count = lax.shift_right_logical(word, byte) & 255
            lists_ref[dest, count] = where + tenant * 1024 + (tenant * tiles + n) * 2048
            one = lax.shift_left(jnp.int32(1), byte)
            return counts[0] + jnp.where(first, one, 0), counts[1] + jnp.where(first, 0, one)

        counts = lax.fori_loop(0, tiles, place, counts, unroll=4)
    for dest in range(8):
        lists_ref[dest, COUNT] = lax.shift_right_logical(counts[dest // 4], (dest % 4) * 8) & 255


def list_tiles(block_index):
    return pl.pallas_call(
        list_kernel,
        out_shape=jax.ShapeDtypeStruct((8, 128), jnp.int32),
        in_specs=[pl.BlockSpec(memory_space=pltpu.SMEM)],
        out_specs=pl.BlockSpec(memory_space=pltpu.SMEM),
        compiler_params=pltpu.CompilerParams(vmem_limit_bytes=1 * MIB),
        cost_estimate=pl.CostEstimate(flops=0, bytes_accessed=8 * MIB, transcendentals=0),
        name="list_tiles",
    )(block_index)


def pick(lists_ref, slab, out_ref, dest, first):
    count = lists_ref[dest, COUNT]

    def one(s, carry):
        at = first + s
        entry = lists_ref[dest, jnp.minimum(at, COUNT)]
        tile = jnp.where(at < count, lax.shift_right_logical(entry, 11), 0)
        out_ref[s] = slab[tile]
        return carry

    lax.fori_loop(0, SLOTS, one, 0, unroll=4)


def send_to(axis):
    def remote(src, dst, s, r, who):
        return pltpu.make_async_remote_copy(
            src_ref=src, dst_ref=dst, send_sem=s, recv_sem=r, device_id={axis: who}, device_id_type=MESH
        )

    return remote


def ring():
    part = lax.axis_index("row")
    core = part % 2
    y = part // 2
    up = ((y + 1) % 4) * 2 + core
    down = ((y + 3) % 4) * 2 + core
    far = ((y + 2) % 4) * 2 + core
    twin = y * 2 + (1 - core)
    return part, up, down, far, twin


def greet(t, up, down, twin):
    barrier = pltpu.get_barrier_semaphore()
    for k in OFFSETS:
        pl.semaphore_signal(barrier, inc=1, device_id={"tenant": (t + k) % 8}, device_id_type=MESH)
    for other in (up, down, twin):
        pl.semaphore_signal(barrier, inc=1, device_id={"row": other}, device_id_type=MESH)
    pl.semaphore_wait(barrier, 10)


def first_exchange_kernel(
    lists_ref, lists, delta, acts, weight, recv, all_lists, base, acts_v,
    slab, outgoing, second, known, weight_v, load_sem,
    z_s, z_r, l_s, l_r, up_s, up_r, dn_s, dn_r, fw_s, fw_r, co_s, co_r,
):
    t = lax.axis_index("tenant")
    part, up, down, far, twin = ring()
    tenant_copy, row_copy = send_to("tenant"), send_to("row")
    loads = [
        pltpu.make_async_copy(
            delta.at[:, pl.ds(pl.multiple_of(part * 16, 16), 16), :], slab, load_sem.at[0]
        ),
        pltpu.make_async_copy(lists, all_lists.at[t], load_sem.at[1]),
        pltpu.make_async_copy(weight, weight_v, load_sem.at[2]),
        pltpu.make_async_copy(acts, acts_v, load_sem.at[3]),
    ]
    for load in loads:
        load.start()
    greet(t, up, down, twin)

    sent = []

    def go(copy):
        copy.start()
        sent.append(copy)
        return copy

    tables = []
    for i, k in enumerate(OFFSETS):
        tables.append(go(tenant_copy(lists, all_lists.at[t], l_s.at[i], l_r.at[i], (t + k) % 8)))
    loads[0].wait()
    z_copies = []
    for i, k in enumerate(OFFSETS):
        dest = (t + k) % 8
        pick(lists_ref, slab, outgoing.at[i], dest, 0)
        copy = tenant_copy(
            outgoing.at[i, pl.ds(0, HALF)], recv.at[part, pl.ds(i * HALF, HALF)], z_s.at[i], z_r.at[i], dest
        )
        if i < AHEAD:
            go(copy)
        z_copies.append(copy)
    for i, k in enumerate(OFFSETS):
        copy = tenant_copy(
            outgoing.at[i, pl.ds(HALF, HALF)], second.at[i], z_s.at[7 + i], z_r.at[7 + i], (t + k) % 8
        )
        if 7 + i < AHEAD:
            go(copy)
        z_copies.append(copy)
    loads[1].wait()
    for table in tables:
        table.wait_recv()
    learn = pltpu.make_async_copy(all_lists, known, load_sem.at[4])
    learn.start()
    learn.wait()

    ups, downs, forwards, twins = {}, {}, {}, []

    def spans(g):
        half = SIZES[g] // 2
        return pl.ds(STARTS[g], half), pl.ds(STARTS[g] + half, half)

    def share(g, n, owner):
        block = recv.at[owner, pl.ds(STARTS[g], SIZES[g])]
        twins.append(go(row_copy(block, block, co_s.at[g, n], co_r.at[g, n], twin)))

    def landed(i):
        z_copies[i].wait_recv()
        if i + AHEAD < 14:
            go(z_copies[i + AHEAD])

    def compact():
        ends = []
        total = jnp.int32(0)
        for k in OFFSETS:
            total = total + jnp.clip(known[(t + 8 - k) % 8, t, COUNT] - HALF, 0, HALF)
            ends.append(total)

        def one(s, carry):
            src, begin = jnp.int32(0), jnp.int32(0)
            for end in ends:
                past = s >= end
                src = src + jnp.where(past, 1, 0)
                begin = jnp.where(past, end, begin)
            recv[part, STARTS[4] + s] = second[jnp.minimum(src, 6), jnp.clip(s - begin, 0, HALF - 1)]
            return carry

        lax.fori_loop(0, SPARE, one, 0, unroll=2)

    def spread(g):
        low, high = spans(g)
        a, b = recv.at[part, low], recv.at[part, high]
        ups[g, 0] = go(row_copy(a, a, up_s.at[g, 0], up_r.at[g, 0], up))
        downs[g, 1] = go(row_copy(b, b, dn_s.at[g, 1], dn_r.at[g, 1], down))
        ups[g, 1] = go(row_copy(b, b, up_s.at[g, 1], up_r.at[g, 1], up))
        downs[g, 0] = go(row_copy(a, a, dn_s.at[g, 0], dn_r.at[g, 0], down))
        share(g, 0, part)

    def neighbours(g):
        low, high = spans(g)
        ups[g, 0].wait_recv()
        a = recv.at[down, low]
        forwards[g, 0] = go(row_copy(a, a, fw_s.at[g, 0], fw_r.at[g, 0], up))
        downs[g, 1].wait_recv()
        b = recv.at[up, high]
        forwards[g, 1] = go(row_copy(b, b, fw_s.at[g, 1], fw_r.at[g, 1], down))
        ups[g, 1].wait_recv()
        share(g, 1, down)
        downs[g, 0].wait_recv()
        share(g, 2, up)

    def opposite(g):
        forwards[g, 0].wait_recv()
        forwards[g, 1].wait_recv()
        share(g, 3, far)

    def multiply(i):
        if i == 0:
            loads[2].wait()
            loads[3].wait()
        rows = pl.ds(i * 256, 256)

        @pl.loop(0, 4)
        def _(c):
            out = jnp.dot(
                acts_v[rows, :],
                weight_v[:, pl.ds(pl.multiple_of(c * 256, 256), 256)],
                preferred_element_type=jnp.float32,
            )
            base[2 * c, rows, :] = out[:, :128]
            base[2 * c + 1, rows, :] = out[:, 128:]

    def arrived(g):
        for i in (2 * g, 2 * g + 1) if g < 3 else (6,):
            landed(i)
        spread(g)

    arrived(0)
    multiply(0)
    arrived(1)
    neighbours(0)
    multiply(1)
    arrived(2)
    opposite(0)
    neighbours(1)
    multiply(2)
    arrived(3)
    neighbours(2)
    opposite(1)
    landed(7)
    landed(8)
    multiply(3)
    neighbours(3)
    opposite(2)
    landed(9)
    landed(10)
    opposite(3)
    landed(11)
    landed(12)
    landed(13)
    compact()
    spread(4)
    neighbours(4)
    opposite(4)
    for copy in twins:
        copy.wait_recv()
    for copy in sent:
        copy.wait_send()


def first_exchange(lists, delta, acts, weight):
    rows, depth = acts.shape
    columns = weight.shape[1]
    any_spec = pl.BlockSpec(memory_space=pl.ANY)
    vmem = pl.BlockSpec(memory_space=pltpu.VMEM)
    dma = pltpu.SemaphoreType.DMA
    return pl.pallas_call(
        first_exchange_kernel,
        out_shape=(
            jax.ShapeDtypeStruct((8, GATHERED, 16, 128), jnp.bfloat16),
            jax.ShapeDtypeStruct((8, 8, 128), jnp.int32),
            jax.ShapeDtypeStruct((columns // 128, rows, 128), jnp.float32),
            jax.ShapeDtypeStruct((rows, depth), jnp.bfloat16),
        ),
        in_specs=[
            pl.BlockSpec(memory_space=pltpu.SMEM),
            any_spec,
            any_spec,
            pl.BlockSpec(memory_space=pltpu.HBM),
            pl.BlockSpec(memory_space=pltpu.HBM),
        ],
        out_specs=(vmem, any_spec, vmem, vmem),
        scratch_shapes=[
            pltpu.VMEM((delta.shape[0], 16, 128), jnp.bfloat16),
            pltpu.VMEM((7, SLOTS, 16, 128), jnp.bfloat16),
        ]
        + [
            pltpu.VMEM((7, HALF, 16, 128), jnp.bfloat16),
            pltpu.SMEM((8, 8, 128), jnp.int32),
            pltpu.VMEM((depth, columns), jnp.bfloat16),
            dma((5,)),
        ]
        + [dma((14,))] * 2
        + [dma((7,))] * 2
        + [dma((5, 2))] * 6
        + [dma((5, 4))] * 2,
        compiler_params=pltpu.CompilerParams(
            collective_id=0, has_side_effects=True, vmem_limit_bytes=28 * MIB
        ),
        name="exchange_tiles_base",
    )(lists, lists, delta, acts, weight)


def exchange_kernel(
    round_ref, lists_ref, delta, unused_weight, recv, slab, outgoing, load_sem,
    z_s, z_r, up_s, up_r, dn_s, dn_r, fw_s, fw_r, co_s, co_r,
):
    t = lax.axis_index("tenant")
    part, up, down, far, twin = ring()
    tenant_copy, row_copy = send_to("tenant"), send_to("row")
    load = pltpu.make_async_copy(
        delta.at[:, pl.ds(pl.multiple_of(part * 16, 16), 16), :], slab, load_sem
    )
    load.start()
    greet(t, up, down, twin)
    load.wait()
    half = SLOTS // 2
    low, high = pl.ds(0, half), pl.ds(half, half)
    for i, k in enumerate(OFFSETS):
        dest = (t + k) % 8
        src = (t + 8 - k) % 8
        pick(lists_ref, slab, outgoing.at[i], dest, round_ref[0] * SLOTS)
        copies = [tenant_copy(outgoing.at[i], recv.at[t, part], z_s.at[i], z_r.at[i], dest)]
        copies[0].start()
        copies[0].wait_recv()

        def go(block, s, r, who):
            copy = row_copy(block, block, s, r, who)
            copy.start()
            copies.append(copy)
            return copy

        block = recv.at[src, part]
        raised = go(block, up_s.at[i], up_r.at[i], up)
        lowered = go(block, dn_s.at[i], dn_r.at[i], down)
        twins = [go(block, co_s.at[i, 0], co_r.at[i, 0], twin)]
        raised.wait_recv()
        lowered.wait_recv()
        one = go(recv.at[src, down, low], fw_s.at[i, 0], fw_r.at[i, 0], up)
        two = go(recv.at[src, up, high], fw_s.at[i, 1], fw_r.at[i, 1], down)
        twins.append(go(recv.at[src, down], co_s.at[i, 1], co_r.at[i, 1], twin))
        twins.append(go(recv.at[src, up], co_s.at[i, 2], co_r.at[i, 2], twin))
        one.wait_recv()
        two.wait_recv()
        twins.append(go(recv.at[src, far], co_s.at[i, 3], co_r.at[i, 3], twin))
        for copy in twins:
            copy.wait_recv()
        for copy in copies:
            copy.wait_send()


def exchange(step, lists, delta, weight):
    dma = pltpu.SemaphoreType.DMA
    return pl.pallas_call(
        exchange_kernel,
        out_shape=jax.ShapeDtypeStruct((8, 8, SLOTS, 16, 128), jnp.bfloat16),
        in_specs=[pl.BlockSpec(memory_space=pltpu.SMEM)] * 2 + [pl.BlockSpec(memory_space=pl.ANY)] * 2,
        out_specs=pl.BlockSpec(memory_space=pltpu.VMEM),
        scratch_shapes=[
            pltpu.VMEM((delta.shape[0], 16, 128), jnp.bfloat16),
            pltpu.VMEM((7, SLOTS, 16, 128), jnp.bfloat16),
            dma,
        ]
        + [dma((7,))] * 6
        + [dma((7, 2))] * 2
        + [dma((7, 4))] * 2,
        compiler_params=pltpu.CompilerParams(
            collective_id=1, has_side_effects=True, vmem_limit_bytes=16 * MIB
        ),
        name="exchange_tiles",
    )(step, lists, delta, weight)


GROUP = 8
CHUNK = 128


def delta_kernel(
    first_round, round_ref, lists_ref, counts_ref, acts_v, own_v, recv, start_ref, out_ref, flag_ref,
    offsets, acc,
):
    t = lax.axis_index("tenant")
    low = round_ref[0] * SLOTS
    rows = acts_v.shape[0]
    longest, over = jnp.int32(0), jnp.int32(0)
    for dest in range(8):
        spare = jnp.int32(0)
        for k in range(1, 8):
            length = lists_ref[(dest + k) % 8, dest, COUNT]
            longest = jnp.maximum(longest, length)
            spare = spare + jnp.maximum(length - HALF, 0)
        over = jnp.maximum(over, spare - SPARE)
    over = jnp.maximum(over, longest - SLOTS)
    flag_ref[...] = jnp.full(flag_ref.shape, jnp.where(over > 0, longest, 0), jnp.int32)
    total = jnp.int32(0)
    for tenant in range(16):
        offsets[tenant] = total
        total = total + counts_ref[0, tenant]
    if first_round:
        acc = start_ref
    else:
        acc[...] = jnp.zeros_like(acc)

    line = lax.broadcasted_iota(jnp.int32, (CHUNK, 128), 0)

    def apply(src, begin, end, tile_of):
        def group(g, carry):
            work = []
            chunks = jnp.int32(0)
            for u in range(GROUP):
                j = begin + g * GROUP + u
                valid = j < end
                j = jnp.minimum(j, end - 1)
                entry = lists_ref[src, t, j]
                tenant = 2 * src + (lax.shift_right_logical(entry, 10) & 1)
                brow = lax.shift_right_logical(entry, 6) & 15
                bcol = entry & 7
                lo = offsets[tenant]
                hi = jnp.where(valid, lo + counts_ref[0, tenant], 0)
                base = lax.shift_right_logical(lo, 4) * 16
                chunks = jnp.maximum(chunks, lax.shift_right_arithmetic(hi - base + CHUNK - 1, 7))
                work.append((j, entry, brow, bcol, lo, hi, base))

            def chunk(i, carry):
                products = []
                for j, entry, brow, bcol, lo, hi, base in work:
                    at = pl.multiple_of(jnp.minimum(base + i * CHUNK, rows - CHUNK), 16)
                    x = acts_v[pl.ds(at, CHUNK), pl.ds(pl.multiple_of(brow * 128, 128), 128)]
                    out = jnp.dot(x, tile_of(j, entry), preferred_element_type=jnp.float32)
                    products.append((at, jnp.maximum(lo, base + i * CHUNK), hi, bcol, out))
                for at, lo, hi, bcol, out in products:
                    keep = (line >= lo - at) & (line < hi - at)
                    acc[bcol, pl.ds(at, CHUNK), :] += jnp.where(keep, out, 0.0)
                return carry

            lax.fori_loop(0, chunks, chunk, 0)
            return carry

        lax.fori_loop(0, lax.div(jnp.maximum(end - begin, 0) + GROUP - 1, GROUP), group, 0)

    begin = jnp.int32(0)
    for i, k in enumerate(OFFSETS):
        src = (t + 8 - k) % 8
        count = lists_ref[src, t, COUNT]
        served = jnp.minimum(count, HALF + jnp.clip(SPARE - begin, 0, HALF))
        later = 7 * HALF + begin - HALF
        begin = begin + jnp.clip(count - HALF, 0, HALF)
        if first_round:
            apply(
                src,
                0,
                served,
                lambda j, entry, i=i, later=later: recv[
                    :, jnp.where(j < HALF, i * HALF, later) + j
                ].reshape(128, 128),
            )
        else:
            apply(
                src,
                jnp.maximum(served, low),
                jnp.minimum(count, low + SLOTS),
                lambda j, entry, src=src: recv[src, :, j - low].reshape(128, 128),
            )
    if first_round:
        apply(t, 0, lists_ref[t, t, COUNT], lambda j, entry: own_v[lax.shift_right_logical(entry, 11)])

    @pl.loop(0, 8)
    def _(i):
        span = pl.ds(pl.multiple_of(i * 128, 128), 128)
        for d in range(4):
            out_ref[d, span, :128] = acc[2 * d, span, :].astype(jnp.bfloat16)
            out_ref[d, span, 128:] = acc[2 * d + 1, span, :].astype(jnp.bfloat16)


def add_delta(step, all_lists, counts, acts, delta, recv, start=None):
    rows = acts.shape[0]
    first_round = start is not None
    smem = pl.BlockSpec(memory_space=pltpu.SMEM)
    vmem = pl.BlockSpec(memory_space=pltpu.VMEM)
    kernel = functools.partial(delta_kernel, first_round)
    if not first_round:

        def kernel(*refs):
            delta_kernel(False, *refs[:6], None, *refs[6:])

    return pl.pallas_call(
        kernel,
        out_shape=(
            jax.ShapeDtypeStruct((4, rows, 256), jnp.bfloat16),
            jax.ShapeDtypeStruct((8, 128), jnp.int32),
        ),
        in_specs=[smem, smem, smem, vmem, vmem, vmem] + [vmem] * first_round,
        out_specs=(vmem, vmem),
        scratch_shapes=[
            pltpu.SMEM((16,), jnp.int32),
            pltpu.VMEM((8, rows, 128) if not first_round else (8, 8, 128), jnp.float32),
        ],
        compiler_params=pltpu.CompilerParams(vmem_limit_bytes=28 * MIB),
        name="add_delta",
    )(step, all_lists, counts, acts, delta, recv, *([start] if first_round else []))


PIECES = 4


def reduce_kernel(
    part, flag, out_ref, longest_ref,
    mine, in_a, in_b, f_a, f_b, g_a, g_b, s_a, s_b, flags, load_sem, send_sem, recv_sem, flag_s, flag_r,
):
    me = lax.axis_index("replica")
    right, left, far = (me + 1) % 4, (me + 3) % 4, (me + 2) % 4
    half = part.shape[1] // 2
    size = half // PIECES

    loads = [
        pltpu.make_async_copy(part.at[right, pl.ds(0, half)], mine.at[0], load_sem.at[0]),
        pltpu.make_async_copy(part.at[left, pl.ds(half, half)], mine.at[1], load_sem.at[1]),
        pltpu.make_async_copy(part.at[me, pl.ds(0, half)], mine.at[2], load_sem.at[2]),
        pltpu.make_async_copy(part.at[me, pl.ds(half, half)], mine.at[3], load_sem.at[3]),
    ]
    for load in loads:
        load.start()
    barrier = pltpu.get_barrier_semaphore()
    for who in (right, left, far):
        pl.semaphore_signal(barrier, inc=1, device_id={"replica": who}, device_id_type=MESH)
    pl.semaphore_wait(barrier, 3)

    started = []

    def send(kind, piece, src, dst, who):
        copy = pltpu.make_async_remote_copy(
            src_ref=src,
            dst_ref=dst,
            send_sem=send_sem.at[kind, piece],
            recv_sem=recv_sem.at[kind, piece],
            device_id={"replica": who},
            device_id_type=MESH,
        )
        copy.start()
        started.append(copy)
        return copy

    ins_a, ins_b, fs_a, fs_b, gs_a, gs_b = [], [], [], [], [], []
    for p in range(PIECES):
        span = pl.ds(p * size, size)
        low, high = pl.ds(p * size, size), pl.ds(half + p * size, size)
        ins_a.append(send(0, p, part.at[far, low], in_a.at[span], right))
        ins_b.append(send(1, p, part.at[far, high], in_b.at[span], left))
    for p in range(PIECES):
        span = pl.ds(p * size, size)
        low, high = pl.ds(p * size, size), pl.ds(half + p * size, size)
        fs_b.append(send(2, p, part.at[right, high], f_b.at[span], right))
        fs_a.append(send(3, p, part.at[left, low], f_a.at[span], left))
    told = []
    for i, who in enumerate((right, left, far)):
        copy = pltpu.make_async_remote_copy(
            src_ref=flag,
            dst_ref=flags.at[i],
            send_sem=flag_s.at[i],
            recv_sem=flag_r.at[i],
            device_id={"replica": who},
            device_id_type=MESH,
        )
        copy.start()
        told.append(copy)
    loads[0].wait()
    loads[1].wait()
    for p in range(PIECES):
        span = pl.ds(p * size, size)
        ins_a[p].wait_recv()
        s_a[span, :] = (mine[0, span, :].astype(jnp.float32) + in_a[span, :].astype(jnp.float32)).astype(jnp.bfloat16)
        gs_a.append(send(4, p, s_a.at[span], g_a.at[span], right))
        ins_b[p].wait_recv()
        s_b[span, :] = (mine[1, span, :].astype(jnp.float32) + in_b[span, :].astype(jnp.float32)).astype(jnp.bfloat16)
        gs_b.append(send(5, p, s_b.at[span], g_b.at[span], left))
    loads[2].wait()
    loads[3].wait()
    for p in range(PIECES):
        span = pl.ds(p * size, size)
        fs_a[p].wait_recv()
        gs_a[p].wait_recv()
        out_ref[pl.ds(p * size, size), :] = (
            mine[2, span, :].astype(jnp.float32) + f_a[span, :].astype(jnp.float32) + g_a[span, :].astype(jnp.float32)
        ).astype(jnp.bfloat16)
        fs_b[p].wait_recv()
        gs_b[p].wait_recv()
        out_ref[pl.ds(half + p * size, size), :] = (
            mine[3, span, :].astype(jnp.float32) + f_b[span, :].astype(jnp.float32) + g_b[span, :].astype(jnp.float32)
        ).astype(jnp.bfloat16)
    for copy in told:
        copy.wait_recv()
    longest = jnp.maximum(jnp.maximum(flags[0], flags[1]), jnp.maximum(flags[2], flag[...]))
    longest_ref[0] = jnp.max(longest)
    for copy in started + told:
        copy.wait_send()


def reduce_blocks(part, flag):
    _, rows, columns = part.shape
    half = rows // 2
    return pl.pallas_call(
        reduce_kernel,
        out_shape=(
            jax.ShapeDtypeStruct((rows, columns), jnp.bfloat16),
            jax.ShapeDtypeStruct((1,), jnp.int32),
        ),
        in_specs=[pl.BlockSpec(memory_space=pl.ANY), pl.BlockSpec(memory_space=pltpu.VMEM)],
        out_specs=(pl.BlockSpec(memory_space=pltpu.VMEM), pl.BlockSpec(memory_space=pltpu.SMEM)),
        scratch_shapes=[pltpu.VMEM((4, half, columns), jnp.bfloat16)]
        + [pltpu.VMEM((half, columns), jnp.bfloat16)] * 8
        + [pltpu.VMEM((3, 8, 128), jnp.int32)]
        + [
            pltpu.SemaphoreType.DMA((4,)),
            pltpu.SemaphoreType.DMA((6, PIECES)),
            pltpu.SemaphoreType.DMA((6, PIECES)),
            pltpu.SemaphoreType.DMA((3,)),
            pltpu.SemaphoreType.DMA((3,)),
        ],
        compiler_params=pltpu.CompilerParams(
            collective_id=2, has_side_effects=True, vmem_limit_bytes=16 * MIB
        ),
        name="reduce_blocks",
    )(part, flag)


def body(acts, base_weight, delta_blocks, block_index, tenant_counts):
    delta = delta_blocks.reshape(-1, 128, 128)
    step = jnp.zeros((1,), jnp.int32)
    lists = list_tiles(block_index)
    recv, all_lists, base, acts_v = first_exchange(lists, delta, acts, base_weight)
    part, flag = add_delta(step, all_lists, tenant_counts, acts_v, delta, recv, base)
    out, longest = reduce_blocks(part, flag)

    def another(n, out):
        step = jnp.full((1,), n - 1, jnp.int32)
        recv = exchange(step, lists, delta, base_weight)
        part, flag = add_delta(step, all_lists, tenant_counts, acts, delta, recv)
        more, _ = reduce_blocks(part, flag)
        return (out.astype(jnp.float32) + more.astype(jnp.float32)).astype(jnp.bfloat16)

    return lax.fori_loop(1, 1 + lax.div(longest[0] + (SLOTS - 1), SLOTS), another, out)


def solution(mesh):
    placed = (
        P("row", "replica"),
        P("replica", "tenant"),
        P("tenant", "replica", None, None),
        P("tenant", "replica"),
        P("row", None),
    )
    return jax.shard_map(
        body, mesh=mesh, in_specs=placed, out_specs=P("row", ("tenant", "replica")), check_vma=False
    )
```

time: 416 us -> 81.7 us (0.20); the launches traced: 408 us -> 81.3 us
  waiting for transfers between devices: 245 us -> 0 us
  local copies, waits for them, and re-layouts: 80.6 us -> 2.56 us
  Pallas kernels: 0 us -> 77.8 us
  matrix products: 38.8 us -> 0 us
  other arithmetic: 29.4 us -> 0 us
  between operations: 13.9 us -> 0.72 us
    reduce_scatter x2 -> x0, waiting for transfers between devices: 245 us -> none  [the longest x1 245 us: body(): lax.psum_scatter(partial_value, ('tenant', 'replica'), scatter_dimension=...]
    pallas_call x0 -> x4, Pallas kernels: none -> 77.8 us  [the longest x1 44.1 us: first_exchange(): pl.pallas_call(first_exchange_kernel, out_shape=(jax.ShapeDtypeStruct((8,...]
    scatter x3 -> x0, local copies, waits for them, and re-layouts: 62.2 us -> none  [body(): partial_value = partial_value.at[target].set(share, mode='drop')]
    dot_general x5 -> x0, matrix products: 38.8 us -> none  [the longest x2 22.4 us: body(): jnp.einsum('cnl,nb->cbl', contrib, onehot, precision=lax.Precision.HIGHEST)]
    convert_element_type x3 -> x0, other arithmetic: 22.3 us -> none  [the longest x2 20.9 us: body(): share = jnp.where(valid[:, None], share, 0.0).astype(jnp.bfloat16)]
    gather x4 -> x0, local copies, waits for them, and re-layouts: 16.2 us -> none  [the longest x2 10.2 us: body(): picked = jnp.take(acts, rowid, axis=0)]
  transfers between devices with their start and end apart: 2 -> 0, of which waited for: 1 -> 0; matrix products, arithmetic and copies ran while one was open for 34% -> 0% of each run, Pallas kernels for 0% -> 0%
where the time goes in v2:
time: 81.7 us; the launch traced here: 81.3 us
  Pallas kernels  77.8 us (95%)
  local copies, waits for them, and re-layouts  2.56 us (3%)
    pallas_call x1, Pallas kernels, first_exchange(): pl.pallas_call(first_exchange_kernel, out_shape=(jax.ShapeDtypeStruct((8,...  44.1 us
    pallas_call x1, Pallas kernels, reduce_blocks(): pl.pallas_call(reduce_kernel, out_shape=(jax.ShapeDtypeStruct((rows, colu...  24.1 us
    pallas_call x1, Pallas kernels, add_delta(): pl.pallas_call(kernel, out_shape=(jax.ShapeDtypeStruct((4, rows, 256), jn...  7.5 us
    unnamed x7, local copies, waits for them, and re-layouts  2.56 us
    pallas_call x1, Pallas kernels, list_tiles(): pl.pallas_call(list_kernel, out_shape=jax.ShapeDtypeStruct((8, 128), jnp....  2.11 us

profile of v2, /device:TPU:1, one launch (start us, length us, event | category | flops | bytes accessed | tf_op | source)
XLA Modules:
  0.0 81.3 jit_solution(5835390570287640166)
XLA Ops:
  0.0 0.0 copy-start
  0.0 0.7 copy-done
  0.7 2.1 %list_tiles.1.lists_ref.lists = s32[8,128]{1,0:T(8,128)S(1)} custom-call(s32[2,52]{1,0:T(2,128)S(1)} %copy-done), custom_call_target="tpu_custom_call" | custom-call | bytes 8388608 | tf_op jit(solution)/shard_map/list_tiles/pallas_call | solution.py:45
  2.8 0.0 copy-start.1
  2.8 0.0 copy-start.3
  2.8 44.1 %exchange_tiles_base.1 = (bf16[8,126,16,128]{3,2,1,0:T(8,128)(2,1)S(1)}, s32[8,8,128]{2,1,0:T(8,128)S(1)}, f32[8,1024,128]{2,1,0:T(8,128)S(1)}, bf16[1024,2048]{1,0:T(8,128)(2,1)S(1)}) custom-call(s32[8,128]{1,0:T(8,128)S(1)} %list_tiles.1.lists_ref.lists, s32[8,128]{1,0:T(8,128)S(1)} %list_tiles.1.lists_ref.lists, bf16[104,128,128]{2,1,0:T(8,128)(2,1)} %bitcast.5, ...), custom_call_target="tpu_custom_call" | custom-call | tf_op jit(solution)/shard_map/exchange_tiles_base/pallas_call | solution.py:273
  46.9 0.0 copy-done.1
  47.0 0.0 copy-done.3
  47.0 7.5 %add_delta.5 = (bf16[4,1024,256]{2,1,0:T(8,128)(2,1)S(1)}, s32[8,128]{1,0:T(8,128)S(1)}) custom-call(s32[1]{0:T(128)} %constant.17.clone.1.round_ref, s32[8,8,128]{2,1,0:T(8,128)S(1)} %get-tuple-element.221.lists_ref, s32[1,16]{1,0:T(1,128)S(1)} %copy-done.3, bf16[1024,2048]{1,0:T(8,128)(2,1)S(1)} %get-tuple-element.127.acts_v, ...), custom_call_target="tpu_custom_call" | custom-call | tf_op jit(solution)/shard_map/add_delta/pallas_call | solution.py:492
  54.5 24.1 %reduce_blocks.5 = (bf16[1024,256]{1,0:T(8,128)(2,1)}, s32[1]{0:T(128)}) custom-call(bf16[4,1024,256]{2,1,0:T(8,128)(2,1)S(1)} %get-tuple-element.130.part, s32[8,128]{1,0:T(8,128)S(1)} %get-tuple-element.131.flag), custom_call_target="tpu_custom_call" | custom-call | tf_op jit(solution)/shard_map/reduce_blocks/pallas_call | solution.py:607
  79.2 0.2 while.12
  79.4 1.9 %copy.13 = bf16[1024,256]{1,0:T(8,128)(2,1)} copy(bf16[1024,256]{1,0:T(8,128)(2,1)} %get-tuple-element.134) | data formatting | bytes 1048576
Async XLA Ops:
  0.0 0.7 copy-start
  2.8 44.1 %copy-start.1 = (bf16[2,52,128,128]{3,2,1,0:T(8,128)(2,1)S(1)}, bf16[2,52,128,128]{3,2,1,0:T(8,128)(2,1)}, u32[]{:S(2)}) copy-start(bf16[2,52,128,128]{3,2,1,0:T(8,128)(2,1)} %param.9) | copy-start | bytes 10223620
  2.8 44.1 %copy-start.3 = (s32[1,16]{1,0:T(1,128)S(1)}, s32[1,16]{1,0:T(1,128)}, u32[]{:S(2)}) copy-start(s32[1,16]{1,0:T(1,128)} %counts_ref.1) | copy-start | bytes 196

commit v3 on v2

--- a/solution.py
+++ b/solution.py
@@ -216,15 +216,15 @@
             loads[3].wait()
         rows = pl.ds(i * 256, 256)
 
-        @pl.loop(0, 4)
+        @pl.loop(0, 2)
         def _(c):
             out = jnp.dot(
                 acts_v[rows, :],
-                weight_v[:, pl.ds(pl.multiple_of(c * 256, 256), 256)],
+                weight_v[:, pl.ds(pl.multiple_of(c * 512, 512), 512)],
                 preferred_element_type=jnp.float32,
             )
-            base[2 * c, rows, :] = out[:, :128]
-            base[2 * c + 1, rows, :] = out[:, 128:]
+            for n in range(4):
+                base[4 * c + n, rows, :] = out[:, n * 128 : (n + 1) * 128]
 
     def arrived(g):
         for i in (2 * g, 2 * g + 1) if g < 3 else (6,):

time: 81.7 us -> 81.7 us (level)
  no operation moved by 1% of the time
where the time goes in v3:
time: 81.7 us; the launch traced here: 82 us
  Pallas kernels  78.5 us (96%)
  local copies, waits for them, and re-layouts  2.56 us (3%)
    pallas_call x1, Pallas kernels, first_exchange(): pl.pallas_call(first_exchange_kernel, out_shape=(jax.ShapeDtypeStruct((8,...  43.9 us
    pallas_call x1, Pallas kernels, reduce_blocks(): pl.pallas_call(reduce_kernel, out_shape=(jax.ShapeDtypeStruct((rows, colu...  24.3 us
    pallas_call x1, Pallas kernels, add_delta(): pl.pallas_call(kernel, out_shape=(jax.ShapeDtypeStruct((4, rows, 256), jn...  8.25 us
    unnamed x7, local copies, waits for them, and re-layouts  2.56 us
    pallas_call x1, Pallas kernels, list_tiles(): pl.pallas_call(list_kernel, out_shape=jax.ShapeDtypeStruct((8, 128), jnp....  2.11 us

profile of v3, /device:TPU:1, one launch (start us, length us, event | category | flops | bytes accessed | tf_op | source)
XLA Modules:
  0.0 82.0 jit_solution(8426036178401934611)
XLA Ops:
  0.0 0.0 copy-start
  0.0 0.7 copy-done
  0.7 2.1 %list_tiles.1.lists_ref.lists = s32[8,128]{1,0:T(8,128)S(1)} custom-call(s32[2,52]{1,0:T(2,128)S(1)} %copy-done), custom_call_target="tpu_custom_call" | custom-call | bytes 8388608 | tf_op jit(solution)/shard_map/list_tiles/pallas_call | solution.py:45
  2.8 0.0 copy-start.1
  2.8 0.0 copy-start.3
  2.8 43.9 %exchange_tiles_base.1 = (bf16[8,126,16,128]{3,2,1,0:T(8,128)(2,1)S(1)}, s32[8,8,128]{2,1,0:T(8,128)S(1)}, f32[8,1024,128]{2,1,0:T(8,128)S(1)}, bf16[1024,2048]{1,0:T(8,128)(2,1)S(1)}) custom-call(s32[8,128]{1,0:T(8,128)S(1)} %list_tiles.1.lists_ref.lists, s32[8,128]{1,0:T(8,128)S(1)} %list_tiles.1.lists_ref.lists, bf16[104,128,128]{2,1,0:T(8,128)(2,1)} %bitcast.5, ...), custom_call_target="tpu_custom_call" | custom-call | tf_op jit(solution)/shard_map/exchange_tiles_base/pallas_call | solution.py:273
  46.7 0.0 copy-done.1
  46.7 0.0 copy-done.3
  46.7 8.2 %add_delta.5 = (bf16[4,1024,256]{2,1,0:T(8,128)(2,1)S(1)}, s32[8,128]{1,0:T(8,128)S(1)}) custom-call(s32[1]{0:T(128)} %constant.17.clone.1.round_ref, s32[8,8,128]{2,1,0:T(8,128)S(1)} %get-tuple-element.221.lists_ref, s32[1,16]{1,0:T(1,128)S(1)} %copy-done.3, bf16[1024,2048]{1,0:T(8,128)(2,1)S(1)} %get-tuple-element.127.acts_v, ...), custom_call_target="tpu_custom_call" | custom-call | tf_op jit(solution)/shard_map/add_delta/pallas_call | solution.py:492
  55.0 24.3 %reduce_blocks.5 = (bf16[1024,256]{1,0:T(8,128)(2,1)}, s32[1]{0:T(128)}) custom-call(bf16[4,1024,256]{2,1,0:T(8,128)(2,1)S(1)} %get-tuple-element.130.part, s32[8,128]{1,0:T(8,128)S(1)} %get-tuple-element.131.flag), custom_call_target="tpu_custom_call" | custom-call | tf_op jit(solution)/shard_map/reduce_blocks/pallas_call | solution.py:607
  79.9 0.2 while.12
  80.1 1.9 %copy.13 = bf16[1024,256]{1,0:T(8,128)(2,1)} copy(bf16[1024,256]{1,0:T(8,128)(2,1)} %get-tuple-element.134) | data formatting | bytes 1048576
Async XLA Ops:
  0.0 0.7 copy-start
  2.8 43.9 %copy-start.1 = (bf16[2,52,128,128]{3,2,1,0:T(8,128)(2,1)S(1)}, bf16[2,52,128,128]{3,2,1,0:T(8,128)(2,1)}, u32[]{:S(2)}) copy-start(bf16[2,52,128,128]{3,2,1,0:T(8,128)(2,1)} %param.9) | copy-start | bytes 10223620
  2.8 43.9 %copy-start.3 = (s32[1,16]{1,0:T(1,128)S(1)}, s32[1,16]{1,0:T(1,128)}, u32[]{:S(2)}) copy-start(s32[1,16]{1,0:T(1,128)} %counts_ref.1) | copy-start | bytes 196
